TPU v7x, 32 devices: a whole 2x2x4 slice. The times are simulated.
32 devices in a mesh: grp: 2 (over y), row: 4 (over z), col: 2 (over x), sub: 2 (over core).
Axes of the slice: x: 2, y: 2, z: 4, core: 2. Of those that a mesh axis runs over, the one named last changes fastest.
Arguments:
- a_blocks: bfloat16 [16, 2, 4, 2, 256, 256], P(('grp', 'row', 'sub'), 'col'), parts along dimension 0, may hold values from 20 to 2000
- block_list: int32 [16, 2, 4, 2], P(('grp', 'row', 'sub'), 'col'), parts along dimension 0, may hold values from 0 to 3, as said below
- block_count: int32 [16, 2, 4], P(('grp', 'row', 'sub'), 'col'), parts along dimension 0, may hold values from 1 to 2
- w_factor: bfloat16 [16, 1024, 256], P(('grp', 'row', 'sub')), parts along dimension 0, may hold values from 0.05 to 4
- h_factor: bfloat16 [256, 4096], P(None, ('grp', 'row', 'col')), parts along dimension 1, may hold values from 0.05 to 4
Outputs:
- w_new: float32 [16, 1024, 256], P(('grp', 'row', 'sub'), 'col'), parts along dimension 0
- h_new: float32 [256, 4096], P(None, ('grp', 'row', 'col')), parts along dimension 1
There are 2 independent parts, one for each index of `grp`. A program takes and returns all parts, laid end to end along the dimension named above; each array names one. Nothing has to cross between parts.
Inputs may be any that keep to these rules, and one draw needn't show every extreme that they name: `block_list`: within one block row and column group the 2 slots name different column blocks.
All inputs are finite; a program needn't handle non-finite values.
Results may differ from a plain program's by a relative error of at most 0.0003.
Values may be sent and summed in bfloat16 or wider, within the bound.
A program may use at most 64 MiB of HBM per device.

v0:
```python
import functools
import jax
import jax.numpy as jnp
from jax import lax
from jax.experimental import pallas as pl
from jax.experimental.pallas import tpu as pltpu
from jax.sharding import PartitionSpec as P

MESH = pl.DeviceIdType.MESH
UNROLL = 8
LEVELS = 65535.0
OFFSET = 32768


def when(condition, action):
    if isinstance(condition, bool):
        if condition:
            action()
    else:
        pl.when(condition)(action)


def each(count, action, first=0):
    if count <= UNROLL:
        for i in range(first, count):
            action(i)
    else:

        def step(i, carry):
            action(i)
            return carry

        lax.fori_loop(first, count, step, 0)


def encode(values, code, scale):
    top = jnp.maximum(jnp.max(values, axis=0, keepdims=True), 1e-30)
    steps = (values * (LEVELS / top) + 0.5).astype(jnp.int32) - OFFSET
    code[...] = steps.astype(jnp.int16)
    scale[...] = jnp.broadcast_to(top * (1.0 / LEVELS), scale.shape)


def decode(code, scale):
    return (code.astype(jnp.int32) + OFFSET).astype(jnp.float32) * scale[0:1, :]


def kernel(
    sizes, a_hbm, lists_hbm, counts_hbm, w_hbm, h_hbm, w_out, h_out,
    lists, counts, a_v, w_v, wt_v, hall, ratios, nw, nh, nhx,
    hq, hq_scale, hq_in, hq_scale_in, wq, wq_scale, wq_in, wq_scale_in,
    hsum, hrecv, wsum, wsrecv, w_inverse, load_sem,
    hs_sem, hr_sem, fs_sem, fr_sem, xs_sem, xr_sem, zs_sem, zr_sem, ys_sem, yr_sem,
    ws_sem, wr_sem, vs_sem, vr_sem, gs_sem, gr_sem, ts_sem, tr_sem, os_sem, or_sem,
):
    n_row, n_col, n_sub = sizes
    row, col, sub = lax.axis_index("row"), lax.axis_index("col"), lax.axis_index("sub")
    other = 1 - sub
    row_blocks, slots, width, _ = a_v.shape
    tile_rows, rank = w_v.shape
    half = rank // n_sub
    share = tile_rows // n_col
    per_share = share // width
    away = row_blocks - per_share
    mine = pl.ds(pl.multiple_of(sub * half, half), half)
    theirs = pl.ds(pl.multiple_of(other * half, half), half)

    def ahead(j):
        return lax.rem(row + j, n_row)

    near = jnp.minimum(row, n_row - 1 - row)
    away_side = jnp.where(2 * row < n_row, 1, -1)

    def target(i):
        step = (i + 1) // 2
        sign = 1 - 2 * (i % 2)
        return row + jnp.where(i <= 2 * near, sign * step, away_side * (i - near))

    load_h = pltpu.make_async_copy(h_hbm, hall.at[row], load_sem.at[0])
    load_w = pltpu.make_async_copy(w_hbm, w_v, load_sem.at[1])
    load_a = pltpu.make_async_copy(a_hbm, a_v, load_sem.at[2])
    load_lists = pltpu.make_async_copy(lists_hbm, lists, load_sem.at[3])
    load_counts = pltpu.make_async_copy(counts_hbm, counts, load_sem.at[4])
    load_w.start()
    load_h.start()
    load_lists.start()
    load_counts.start()
    load_a.start()

    barrier = pltpu.get_barrier_semaphore()

    def greet(i):
        jr, js = i // n_sub, i % n_sub
        pl.semaphore_signal(
            barrier, inc=1, device_id={"row": ahead(jr), "sub": lax.rem(sub + js, n_sub)},
            device_id_type=MESH,
        )

    each(n_row * n_sub, greet, 1)

    def greet_col(j):
        pl.semaphore_signal(
            barrier, inc=1, device_id={"col": lax.rem(col + j, n_col)}, device_id_type=MESH
        )

    each(n_col, greet_col, 1)
    pl.semaphore_wait(barrier, n_row * n_sub - 1 + n_col - 1)

    def h_copy(i):
        return pltpu.make_async_remote_copy(
            src_ref=h_hbm.at[mine], dst_ref=hall.at[row, mine],
            send_sem=hs_sem.at[i], recv_sem=hr_sem.at[row],
            device_id={"row": target(i)}, device_id_type=MESH,
        )

    def h_arrival(i):
        return pltpu.make_async_remote_copy(
            src_ref=h_hbm.at[mine], dst_ref=hall.at[target(i), mine],
            send_sem=hs_sem.at[i], recv_sem=hr_sem.at[target(i)],
            device_id={"row": target(i)}, device_id_type=MESH,
        )

    def forward(i, part):
        return pltpu.make_async_remote_copy(
            src_ref=hall.at[target(i), part], dst_ref=hall.at[target(i), part],
            send_sem=fs_sem.at[i], recv_sem=fr_sem.at[i],
            device_id={"sub": other}, device_id_type=MESH,
        )

    def w_sum_copy(i):
        jr, js = i // n_sub, i % n_sub
        return pltpu.make_async_remote_copy(
            src_ref=wsum, dst_ref=wsrecv.at[i],
            send_sem=ts_sem.at[i], recv_sem=tr_sem.at[i],
            device_id={"row": ahead(jr), "sub": lax.rem(sub + js, n_sub)}, device_id_type=MESH,
        )

    def swap(j):
        return pltpu.make_async_remote_copy(
            src_ref=nh.at[j, theirs], dst_ref=nhx.at[j],
            send_sem=xs_sem.at[j], recv_sem=xr_sem.at[j],
            device_id={"sub": other}, device_id_type=MESH,
        )

    def h_numer_copy(i):
        return pltpu.make_async_remote_copy(
            src_ref=hq.at[i], dst_ref=hq_in.at[row],
            send_sem=zs_sem.at[i], recv_sem=zr_sem.at[row],
            device_id={"row": target(i)}, device_id_type=MESH,
        )

    def h_scale_copy(i):
        return pltpu.make_async_remote_copy(
            src_ref=hq_scale.at[i], dst_ref=hq_scale_in.at[row],
            send_sem=ys_sem.at[i], recv_sem=yr_sem.at[row],
            device_id={"row": target(i)}, device_id_type=MESH,
        )

    def h_numer_arrival(i):
        return pltpu.make_async_remote_copy(
            src_ref=hq.at[i], dst_ref=hq_in.at[target(i)],
            send_sem=zs_sem.at[i], recv_sem=zr_sem.at[target(i)],
            device_id={"row": target(i)}, device_id_type=MESH,
        )

    def h_scale_arrival(i):
        return pltpu.make_async_remote_copy(
            src_ref=hq_scale.at[i], dst_ref=hq_scale_in.at[target(i)],
            send_sem=ys_sem.at[i], recv_sem=yr_sem.at[target(i)],
            device_id={"row": target(i)}, device_id_type=MESH,
        )

    def w_numer_copy(i):
        return pltpu.make_async_remote_copy(
            src_ref=wq.at[i], dst_ref=wq_in.at[i],
            send_sem=ws_sem.at[i], recv_sem=wr_sem.at[i],
            device_id={"col": lax.rem(col + 1 + i // per_share, n_col)}, device_id_type=MESH,
        )

    def w_scale_copy(i):
        return pltpu.make_async_remote_copy(
            src_ref=wq_scale.at[i], dst_ref=wq_scale_in.at[i],
            send_sem=vs_sem.at[i], recv_sem=vr_sem.at[i],
            device_id={"col": lax.rem(col + 1 + i // per_share, n_col)}, device_id_type=MESH,
        )

    def h_sum_copy(j):
        return pltpu.make_async_remote_copy(
            src_ref=hsum, dst_ref=hrecv.at[j],
            send_sem=gs_sem.at[j], recv_sem=gr_sem.at[j],
            device_id={"col": lax.rem(col + j, n_col)}, device_id_type=MESH,
        )

    each(n_row, lambda i: h_copy(i).start(), 1)

    load_w.wait()
    wsum[...] = jnp.dot(
        jnp.ones((8, tile_rows), jnp.bfloat16), w_v[...], preferred_element_type=jnp.float32
    )
    each(n_row * n_sub, lambda i: w_sum_copy(i).start(), 1)
    wt_v[...] = w_v[...].T
    load_h.wait()
    load_a.wait()

    load_lists.wait()
    load_counts.wait()

    def add_w_sums():
        def add(i):
            w_sum_copy(i).wait()
            wsrecv[0] = wsrecv[0] + wsrecv[i]

        wsrecv[0] = wsum[...]
        each(n_row * n_sub, add, 1)
        down = lax.broadcasted_iota(jnp.int32, (half, rank), 0) + sub * half
        along = lax.broadcasted_iota(jnp.int32, (half, rank), 1)
        total = jnp.sum(
            jnp.where(down == along, wsrecv[0, 0:1, :], 0.0), axis=1, keepdims=True
        )
        w_inverse[...] = jnp.broadcast_to(1.0 / total, (half, width))

    def add_pair(j):
        swap(j).wait()
        numer = nhx[j] + nh[j, mine, :]
        return hall[target(j), mine, :].astype(jnp.float32) * numer * w_inverse[...]

    def send_numer(j):
        encode(add_pair(j), hq.at[j], hq_scale.at[j])
        h_numer_copy(j).start()
        h_scale_copy(j).start()

    def receive(i):
        h_arrival(i).wait_recv()
        forward(i, mine).start()

    def turn(i):
        first = i == 0
        last = i == n_row - 1
        when(i > 0, lambda: forward(i, theirs).wait_recv())
        block = target(i)
        h_block = hall[block]
        product = jnp.dot(w_v[...], h_block, preferred_element_type=jnp.float32)
        for brow in range(row_blocks):
            position = jnp.int32(0)
            live = jnp.float32(0)
            for slot in range(slots):
                match = (lists[slot, brow] == block) & (slot < counts[brow])
                position = jnp.where(match, slot, position)
                live = jnp.where(match, jnp.float32(1), live)
            rows = slice(brow * width, (brow + 1) * width)
            entries = a_v[brow, position].astype(jnp.float32) * live
            ratios[rows, :] = (entries / product[rows]).astype(jnp.bfloat16)
        if isinstance(i, int):
            when(0 < i < n_row - 1, lambda: receive(i + 1))
        else:
            when((0 < i) & (i < n_row - 1), lambda: receive(i + 1))
        part_w = lax.dot_general(
            ratios[...], h_block, (((1,), (1,)), ((), ())), preferred_element_type=jnp.float32
        )
        part_h = lax.dot_general(
            jnp.ones((8, width), jnp.bfloat16), h_block, (((1,), (1,)), ((), ())),
            preferred_element_type=jnp.float32,
        )
        if isinstance(i, int) and first:
            nw[...] = part_w
            hsum[...] = part_h
        else:
            nw[...] = nw[...] + part_w
            hsum[...] = hsum[...] + part_h

        def send_w():
            for place in range(away):
                brow = lax.rem((col + 1) * per_share + place, row_blocks)
                rows = pl.ds(pl.multiple_of(brow * width, width), width)
                numer = w_v[rows, :].astype(jnp.float32) * nw[rows, :]
                encode(numer, wq.at[place], wq_scale.at[place])
                w_numer_copy(place).start()
                w_scale_copy(place).start()
            each(n_col, lambda k: h_sum_copy(k).start(), 1)

        when(last, send_w)
        when(i > 1, lambda: send_numer(i - 1))
        nh[i] = jnp.dot(wt_v[...], ratios[...], preferred_element_type=jnp.float32)
        swap(i).start()

        def between():
            receive(1)
            add_w_sums()
            h_out[mine, :] = add_pair(0)

        when(first, between)

    if n_row > UNROLL:
        nw[...] = jnp.zeros_like(nw)
        hsum[...] = jnp.zeros_like(hsum)
    each(n_row, turn)
    send_numer(n_row - 1)
    own = pl.ds(pl.multiple_of(col * share, share), share)
    w_out[...] = w_v[own, :].astype(jnp.float32) * nw[own, :]

    def add_h_numer(i):
        h_numer_arrival(i).wait_recv()
        h_scale_arrival(i).wait_recv()
        h_out[mine, :] = h_out[mine, :] + decode(hq_in[target(i)], hq_scale_in[target(i)])

    each(n_row, add_h_numer, 1)
    h_finish = pltpu.make_async_remote_copy(
        src_ref=h_out.at[mine], dst_ref=h_out.at[mine], send_sem=os_sem, recv_sem=or_sem,
        device_id={"sub": other}, device_id_type=MESH,
    )
    h_finish.start()

    each(n_col, lambda j: h_sum_copy(j).wait(), 1)
    h_total = hsum[0:1, :]
    for j in range(1, n_col):
        h_total = h_total + hrecv[j, 0:1, :]
    for i in range(away):
        rows = pl.ds(i % per_share * width, width)
        w_numer_copy(i).wait()
        w_scale_copy(i).wait()
        total = w_out[rows, :] + decode(wq_in[i], wq_scale_in[i])
        w_out[rows, :] = total / h_total if i >= away - per_share else total

    def settle(j):
        h_copy(j).wait_send()
        h_numer_copy(j).wait_send()
        h_scale_copy(j).wait_send()
        forward(j, mine).wait_send()

    each(n_row, settle, 1)
    h_finish.wait_send()
    h_arrived = pltpu.make_async_remote_copy(
        src_ref=h_out.at[mine], dst_ref=h_out.at[theirs], send_sem=os_sem, recv_sem=or_sem,
        device_id={"sub": other}, device_id_type=MESH,
    )
    h_arrived.wait_recv()


def body(a_blocks, block_list, block_count, w_factor, h_factor):
    n_row, n_col, n_sub = (lax.axis_size(axis) for axis in ("row", "col", "sub"))
    a, lists, counts, w = a_blocks[0, 0], block_list[0, 0], block_count[0, 0], w_factor[0]
    tile_rows, rank = w.shape
    width = h_factor.shape[1]
    half = rank // n_sub
    share = tile_rows // n_col
    away = (tile_rows - share) // width
    f32, bf16, i16, i32 = jnp.float32, jnp.bfloat16, jnp.int16, jnp.int32
    dma = pltpu.SemaphoreType.DMA
    vmem, smem = pltpu.VMEM, pltpu.SMEM
    lists = lists.T
    w_new, h_new = pl.pallas_call(
        functools.partial(kernel, (n_row, n_col, n_sub)),
        out_shape=(
            jax.ShapeDtypeStruct((share, rank), f32),
            jax.ShapeDtypeStruct((rank, width), f32),
        ),
        in_specs=[pl.BlockSpec(memory_space=pltpu.HBM)] * 5,
        out_specs=(pl.BlockSpec(memory_space=vmem), pl.BlockSpec(memory_space=vmem)),
        scratch_shapes=[
            smem(lists.shape, i32),
            smem(counts.shape, i32),
            vmem(a.shape, bf16),
            vmem(w.shape, bf16),
            vmem((rank, tile_rows), bf16),
            vmem((n_row, rank, width), bf16),
            vmem((tile_rows, width), bf16),
            vmem((tile_rows, rank), f32),
            vmem((n_row, rank, width), f32),
            vmem((n_row, half, width), f32),
            vmem((n_row, half, width), i16),
            vmem((n_row, 8, width), f32),
            vmem((n_row, half, width), i16),
            vmem((n_row, 8, width), f32),
            vmem((away, width, rank), i16),
            vmem((away, 8, rank), f32),
            vmem((away, width, rank), i16),
            vmem((away, 8, rank), f32),
            vmem((8, rank), f32),
            vmem((n_col, 8, rank), f32),
            vmem((8, rank), f32),
            vmem((n_row * n_sub, 8, rank), f32),
            vmem((half, width), f32),
            dma((5,)),
            *[dma((n_row,))] * 10,
            *[dma((away,))] * 4,
            *[dma((n_col,))] * 2,
            *[dma((n_row * n_sub,))] * 2,
            dma,
            dma,
        ],
        compiler_params=pltpu.CompilerParams(
            collective_id=0, has_side_effects=True, vmem_limit_bytes=63 * 2**20
        ),
    )(a, lists, counts, w, h_factor)
    return w_new[None], h_new


def solution(mesh):
    placed = (
        P(("grp", "row", "sub"), "col", None, None, None, None),
        P(("grp", "row", "sub"), "col", None, None),
        P(("grp", "row", "sub"), "col", None),
        P(("grp", "row", "sub"), None, None),
        P(None, ("grp", "row", "col")),
    )
    return jax.shard_map(
        body,
        mesh=mesh,
        in_specs=placed,
        out_specs=(P(("grp", "row", "sub"), "col", None), P(None, ("grp", "row", "col"))),
        check_vma=False,
    )
```

profile of v0, /device:TPU:0, one launch (start us, length us, event | category | flops | bytes accessed | tf_op | source)
XLA Modules:
  0.0 32.6 jit_solution(15532147913703165786)
XLA Ops:
  0.6 29.3 %shard_map.68 = (f32[512,256]{1,0:T(8,128)}, f32[256,256]{1,0:T(8,128)}) custom-call(bf16[4,2,256,256]{3,2,1,0:T(8,128)(2,1)} %bitcast.7, s32[2,4]{1,0:T(2,128)} %bitcast.10, s32[4]{0:T(128)} %bitcast.11, bf16[1024,256]{1,0:T(8,128)(2,1)} %bitcast.8, bf16[256,256]{1,0:T(8,128)(2,1)} %h_hbm.1), custom_call_target="tpu_custom_call" | custom-call | tf_op jit(solution)/shard_map/pallas_call | solution.py:350
  30.0 0.0 copy-start
  30.0 1.9 %copy.9 = f32[1,512,256]{2,1,0:T(8,128)} copy(f32[1,512,256]{2,1,0:T(8,128)} %bitcast.9) | data formatting | bytes 1048576
  31.9 0.0 copy-done
  31.9 0.7 %copy.10 = f32[256,256]{1,0:T(8,128)} copy(f32[256,256]{1,0:T(8,128)S(1)} %copy-done) | data formatting | bytes 524288
Async XLA Ops:
  30.0 1.9 %copy-start = (f32[256,256]{1,0:T(8,128)S(1)}, f32[256,256]{1,0:T(8,128)}, u32[]{:S(2)}) copy-start(f32[256,256]{1,0:T(8,128)} %get-tuple-element.9) | copy-start | bytes 786436
where the time goes:
time: 32.7 us; the launch traced here: 32.6 us
  Pallas kernels  29.3 us (90%)
  local copies, waits for them, and re-layouts  2.62 us (8%)
  between operations  0.65 us (2%)
    pallas_call x1, Pallas kernels, body(): pl.pallas_call(functools.partial(kernel, (n_row, n_col, n_sub)), out_shap...  29.3 us
    unnamed x4, local copies, waits for them, and re-layouts  2.62 us

commit v1 on v0

--- a/solution.py
+++ b/solution.py
@@ -7,7 +7,7 @@
 from jax.sharding import PartitionSpec as P
 
 MESH = pl.DeviceIdType.MESH
-UNROLL = 8
+UNROLL = 2
 LEVELS = 65535.0
 OFFSET = 32768
 

time: 32.7 us -> 32.3 us (0.988)
  Pallas kernels: 29.3 us -> 28.8 us
    pallas_call x1, Pallas kernels: 29.3 us -> 28.8 us  [body(): pl.pallas_call(functools.partial(kernel, (n_row, n_col, n_sub)), out_shap...]
where the time goes in v1:
time: 32.3 us; the launch traced here: 32.1 us
  Pallas kernels  28.8 us (89%)
  local copies, waits for them, and re-layouts  2.62 us (8%)
  between operations  0.65 us (2%)
    pallas_call x1, Pallas kernels, body(): pl.pallas_call(functools.partial(kernel, (n_row, n_col, n_sub)), out_shap...  28.8 us
    unnamed x4, local copies, waits for them, and re-layouts  2.62 us

profile of v1, /device:TPU:0, one launch (start us, length us, event | category | flops | bytes accessed | tf_op | source)
XLA Modules:
  0.0 32.1 jit_solution(13321744511001783974)
XLA Ops:
  0.6 28.8 %shard_map.68 = (f32[512,256]{1,0:T(8,128)}, f32[256,256]{1,0:T(8,128)}) custom-call(bf16[4,2,256,256]{3,2,1,0:T(8,128)(2,1)} %bitcast.7, s32[2,4]{1,0:T(2,128)} %bitcast.10, s32[4]{0:T(128)} %bitcast.11, bf16[1024,256]{1,0:T(8,128)(2,1)} %bitcast.8, bf16[256,256]{1,0:T(8,128)(2,1)} %h_hbm.1), custom_call_target="tpu_custom_call" | custom-call | tf_op jit(solution)/shard_map/pallas_call | solution.py:350
  29.5 0.0 copy-start
  29.5 1.9 %copy.9 = f32[1,512,256]{2,1,0:T(8,128)} copy(f32[1,512,256]{2,1,0:T(8,128)} %bitcast.9) | data formatting | bytes 1048576
  31.4 0.0 copy-done
  31.4 0.7 %copy.10 = f32[256,256]{1,0:T(8,128)} copy(f32[256,256]{1,0:T(8,128)S(1)} %copy-done) | data formatting | bytes 524288
Async XLA Ops:
  29.5 1.9 %copy-start = (f32[256,256]{1,0:T(8,128)S(1)}, f32[256,256]{1,0:T(8,128)}, u32[]{:S(2)}) copy-start(f32[256,256]{1,0:T(8,128)} %get-tuple-element.9) | copy-start | bytes 786436

commit v2 on v1

--- a/solution.py
+++ b/solution.py
@@ -10,6 +10,8 @@
 UNROLL = 2
 LEVELS = 65535.0
 OFFSET = 32768
+LIMIT = 63 * 2**20
+PIECES = 4
 
 
 def when(condition, action):
@@ -333,6 +335,21 @@
         device_id={"sub": other}, device_id_type=MESH,
     )
     h_arrived.wait_recv()
+
+
+def place_outputs(w_in, h_in, w_out, h_out, sem):
+    copies = []
+    for source, to in ((w_in, w_out), (h_in, h_out)):
+        rows = source.shape[0] // PIECES
+        for piece in range(PIECES):
+            part = pl.ds(piece * rows, rows)
+            copies.append(
+                pltpu.make_async_copy(source.at[part], to.at[part], sem.at[len(copies)])
+            )
+    for copy in copies:
+        copy.start()
+    for copy in copies:
+        copy.wait()
 
 
 def body(a_blocks, block_list, block_count, w_factor, h_factor):
@@ -388,9 +405,20 @@
             dma,
         ],
         compiler_params=pltpu.CompilerParams(
-            collective_id=0, has_side_effects=True, vmem_limit_bytes=63 * 2**20
+            collective_id=0, has_side_effects=True, vmem_limit_bytes=LIMIT
         ),
     )(a, lists, counts, w, h_factor)
+    w_new, h_new = pl.pallas_call(
+        place_outputs,
+        out_shape=(
+            jax.ShapeDtypeStruct(w_new.shape, f32),
+            jax.ShapeDtypeStruct(h_new.shape, f32),
+        ),
+        in_specs=[pl.BlockSpec(memory_space=pl.ANY)] * 2,
+        out_specs=(pl.BlockSpec(memory_space=pl.ANY),) * 2,
+        scratch_shapes=[dma((2 * PIECES,))],
+        compiler_params=pltpu.CompilerParams(vmem_limit_bytes=LIMIT),
+    )(w_new, h_new)
     return w_new[None], h_new
 
 

time: 32.3 us -> 54.6 us (1.69)
  Pallas kernels: 28.8 us -> 53.8 us
  local copies, waits for them, and re-layouts: 2.62 us -> 0 us
    pallas_call x0 -> x1, Pallas kernels: none -> 25 us  [body(): pl.pallas_call(place_outputs, out_shape=(jax.ShapeDtypeStruct(w_new.shape...]
    unnamed x4 -> x0, local copies, waits for them, and re-layouts: 2.62 us -> none
where the time goes in v2:
time: 54.6 us; the launch traced here: 54.5 us
  Pallas kernels  53.8 us (99%)
  between operations  0.64 us (1%)
    pallas_call x1, Pallas kernels, body(): pl.pallas_call(functools.partial(kernel, (n_row, n_col, n_sub)), out_shap...  28.8 us
    pallas_call x1, Pallas kernels, body(): pl.pallas_call(place_outputs, out_shape=(jax.ShapeDtypeStruct(w_new.shape...  25 us

profile of v2, /device:TPU:0, one launch (start us, length us, event | category | flops | bytes accessed | tf_op | source)
XLA Modules:
  0.0 54.5 jit_solution(7468985518991141977)
XLA Ops:
  0.6 28.8 %shard_map.68 = (f32[512,256]{1,0:T(8,128)}, f32[256,256]{1,0:T(8,128)}) custom-call(bf16[4,2,256,256]{3,2,1,0:T(8,128)(2,1)} %bitcast.7, s32[2,4]{1,0:T(2,128)} %bitcast.9, s32[4]{0:T(128)} %bitcast.10, bf16[1024,256]{1,0:T(8,128)(2,1)} %bitcast.8, bf16[256,256]{1,0:T(8,128)(2,1)} %h_hbm.1), custom_call_target="tpu_custom_call" | custom-call | tf_op jit(solution)/shard_map/pallas_call | solution.py:367
  29.5 25.0 %shard_map.69 = (f32[512,256]{1,0:T(8,128)}, f32[256,256]{1,0:T(8,128)}) custom-call(f32[512,256]{1,0:T(8,128)} %get-tuple-element.6.w_in, f32[256,256]{1,0:T(8,128)} %get-tuple-element.7.h_in), custom_call_target="tpu_custom_call" | custom-call | tf_op jit(solution)/shard_map/pallas_call | solution.py:411

commit v3 on v2

--- a/solution.py
+++ b/solution.py
@@ -109,14 +109,14 @@
 
     def h_copy(i):
         return pltpu.make_async_remote_copy(
-            src_ref=h_hbm.at[mine], dst_ref=hall.at[row, mine],
+            src_ref=hall.at[row, mine], dst_ref=hall.at[row, mine],
             send_sem=hs_sem.at[i], recv_sem=hr_sem.at[row],
             device_id={"row": target(i)}, device_id_type=MESH,
         )
 
     def h_arrival(i):
         return pltpu.make_async_remote_copy(
-            src_ref=h_hbm.at[mine], dst_ref=hall.at[target(i), mine],
+            src_ref=hall.at[row, mine], dst_ref=hall.at[target(i), mine],
             send_sem=hs_sem.at[i], recv_sem=hr_sem.at[target(i)],
             device_id={"row": target(i)}, device_id_type=MESH,
         )
@@ -192,6 +192,7 @@
             device_id={"col": lax.rem(col + j, n_col)}, device_id_type=MESH,
         )
 
+    load_h.wait()
     each(n_row, lambda i: h_copy(i).start(), 1)
 
     load_w.wait()
@@ -200,7 +201,6 @@
     )
     each(n_row * n_sub, lambda i: w_sum_copy(i).start(), 1)
     wt_v[...] = w_v[...].T
-    load_h.wait()
     load_a.wait()
 
     load_lists.wait()
@@ -337,19 +337,24 @@
     h_arrived.wait_recv()
 
 
-def place_outputs(w_in, h_in, w_out, h_out, sem):
-    copies = []
-    for source, to in ((w_in, w_out), (h_in, h_out)):
+def place_outputs(w_in, h_in, w_out, h_out, w_held, h_held, in_sem, out_sem):
+    inward, outward = [], []
+    for source, held, to in ((h_in, h_held, h_out), (w_in, w_held, w_out)):
         rows = source.shape[0] // PIECES
         for piece in range(PIECES):
             part = pl.ds(piece * rows, rows)
-            copies.append(
-                pltpu.make_async_copy(source.at[part], to.at[part], sem.at[len(copies)])
+            n = len(inward)
+            inward.append(
+                pltpu.make_async_copy(source.at[part], held.at[part], in_sem.at[n])
             )
-    for copy in copies:
+            outward.append(pltpu.make_async_copy(held.at[part], to.at[part], out_sem.at[n]))
+    for copy in inward:
         copy.start()
-    for copy in copies:
+    for copy, onward in zip(inward, outward):
         copy.wait()
+        onward.start()
+    for onward in outward:
+        onward.wait()
 
 
 def body(a_blocks, block_list, block_count, w_factor, h_factor):
@@ -416,7 +421,12 @@
         ),
         in_specs=[pl.BlockSpec(memory_space=pl.ANY)] * 2,
         out_specs=(pl.BlockSpec(memory_space=pl.ANY),) * 2,
-        scratch_shapes=[dma((2 * PIECES,))],
+        scratch_shapes=[
+            vmem(w_new.shape, f32),
+            vmem(h_new.shape, f32),
+            dma((2 * PIECES,)),
+            dma((2 * PIECES,)),
+        ],
         compiler_params=pltpu.CompilerParams(vmem_limit_bytes=LIMIT),
     )(w_new, h_new)
     return w_new[None], h_new

time: 54.6 us -> 31.4 us (0.58)
  Pallas kernels: 53.8 us -> 30.6 us
    pallas_call x1, Pallas kernels: 25 us -> 2.01 us  [body(): pl.pallas_call(place_outputs, out_shape=(jax.ShapeDtypeStruct(w_new.shape...]
where the time goes in v3:
time: 31.4 us; the launch traced here: 31.3 us
  Pallas kernels  30.6 us (97%)
  between operations  0.64 us (2%)
    pallas_call x1, Pallas kernels, body(): pl.pallas_call(functools.partial(kernel, (n_row, n_col, n_sub)), out_shap...  28.6 us
    pallas_call x1, Pallas kernels, body(): pl.pallas_call(place_outputs, out_shape=(jax.ShapeDtypeStruct(w_new.shape...  2.01 us

profile of v3, /device:TPU:0, one launch (start us, length us, event | category | flops | bytes accessed | tf_op | source)
XLA Modules:
  0.0 31.3 jit_solution(6987151424767618913)
XLA Ops:
  0.6 28.6 %shard_map.68 = (f32[512,256]{1,0:T(8,128)}, f32[256,256]{1,0:T(8,128)}) custom-call(bf16[4,2,256,256]{3,2,1,0:T(8,128)(2,1)} %bitcast.7, s32[2,4]{1,0:T(2,128)} %bitcast.9, s32[4]{0:T(128)} %bitcast.10, bf16[1024,256]{1,0:T(8,128)(2,1)} %bitcast.8, bf16[256,256]{1,0:T(8,128)(2,1)} %h_hbm.1), custom_call_target="tpu_custom_call" | custom-call | tf_op jit(solution)/shard_map/pallas_call | solution.py:372
  29.2 2.0 %shard_map.69 = (f32[512,256]{1,0:T(8,128)}, f32[256,256]{1,0:T(8,128)}) custom-call(f32[512,256]{1,0:T(8,128)} %get-tuple-element.6.w_in, f32[256,256]{1,0:T(8,128)} %get-tuple-element.7.h_in), custom_call_target="tpu_custom_call" | custom-call | tf_op jit(solution)/shard_map/pallas_call | solution.py:416

commit v4 on v2

--- a/solution.py
+++ b/solution.py
@@ -10,7 +10,7 @@
 UNROLL = 2
 LEVELS = 65535.0
 OFFSET = 32768
-LIMIT = 63 * 2**20
+LIMIT = 53 * 2**20
 PIECES = 4
 
 
@@ -109,14 +109,14 @@
 
     def h_copy(i):
         return pltpu.make_async_remote_copy(
-            src_ref=h_hbm.at[mine], dst_ref=hall.at[row, mine],
+            src_ref=hall.at[row, mine], dst_ref=hall.at[row, mine],
             send_sem=hs_sem.at[i], recv_sem=hr_sem.at[row],
             device_id={"row": target(i)}, device_id_type=MESH,
         )
 
     def h_arrival(i):
         return pltpu.make_async_remote_copy(
-            src_ref=h_hbm.at[mine], dst_ref=hall.at[target(i), mine],
+            src_ref=hall.at[row, mine], dst_ref=hall.at[target(i), mine],
             send_sem=hs_sem.at[i], recv_sem=hr_sem.at[target(i)],
             device_id={"row": target(i)}, device_id_type=MESH,
         )
@@ -192,6 +192,7 @@
             device_id={"col": lax.rem(col + j, n_col)}, device_id_type=MESH,
         )
 
+    load_h.wait()
     each(n_row, lambda i: h_copy(i).start(), 1)
 
     load_w.wait()
@@ -200,7 +201,6 @@
     )
     each(n_row * n_sub, lambda i: w_sum_copy(i).start(), 1)
     wt_v[...] = w_v[...].T
-    load_h.wait()
     load_a.wait()
 
     load_lists.wait()

time: 54.6 us -> 31.1 us (0.57)
  Pallas kernels: 53.8 us -> 28.8 us
  local copies, waits for them, and re-layouts: 0 us -> 1.57 us
    pallas_call x1, Pallas kernels: 25 us -> 0.94 us  [body(): pl.pallas_call(place_outputs, out_shape=(jax.ShapeDtypeStruct(w_new.shape...]
    unnamed x0 -> x6, local copies, waits for them, and re-layouts: none -> 1.57 us
    pallas_call x1, Pallas kernels: 28.8 us -> 27.8 us  [body(): pl.pallas_call(functools.partial(kernel, (n_row, n_col, n_sub)), out_shap...]
where the time goes in v4:
time: 31.1 us; the launch traced here: 31 us
  Pallas kernels  28.8 us (93%)
  local copies, waits for them, and re-layouts  1.57 us (5%)
  between operations  0.66 us (2%)
    pallas_call x1, Pallas kernels, body(): pl.pallas_call(functools.partial(kernel, (n_row, n_col, n_sub)), out_shap...  27.8 us
    unnamed x6, local copies, waits for them, and re-layouts  1.57 us
    pallas_call x1, Pallas kernels, body(): pl.pallas_call(place_outputs, out_shape=(jax.ShapeDtypeStruct(w_new.shape...  0.94 us

profile of v4, /device:TPU:0, one launch (start us, length us, event | category | flops | bytes accessed | tf_op | source)
XLA Modules:
  0.0 31.0 jit_solution(12083327452235814176)
XLA Ops:
  0.6 0.0 copy-start.1
  0.6 0.0 copy-start.2
  0.7 0.7 %copy-done.1 = s32[1,1,4,2]{2,3,1,0:T(2,128)S(1)} copy-done((s32[1,1,4,2]{2,3,1,0:T(2,128)S(1)}, s32[1,1,4,2]{2,3,1,0:T(2,128)}, u32[]{:S(2)}) %copy-start.1) | copy-done | bytes 56
  1.3 0.0 copy-done.2
  1.3 0.0 copy-start
  1.3 0.9 %copy-done = bf16[256,256]{1,0:T(8,128)(2,1)S(1)} copy-done((bf16[256,256]{1,0:T(8,128)(2,1)S(1)}, bf16[256,256]{1,0:T(8,128)(2,1)}, u32[]{:S(2)}) %copy-start) | copy-done | bytes 131096
  2.2 27.8 %shard_map.68 = (f32[512,256]{1,0:T(8,128)S(1)}, f32[256,256]{1,0:T(8,128)S(1)}) custom-call(bf16[4,2,256,256]{3,2,1,0:T(8,128)(2,1)} %bitcast.9, s32[2,4]{1,0:T(2,128)S(1)} %bitcast.7, s32[4]{0:T(128)S(1)} %bitcast.8, bf16[1024,256]{1,0:T(8,128)(2,1)} %bitcast.10, bf16[256,256]{1,0:T(8,128)(2,1)S(1)} %copy-done), custom_call_target="tpu_custom_call" | custom-call | tf_op jit(solution)/shard_map/pallas_call | solution.py:367
  30.0 0.9 %shard_map.69 = (f32[512,256]{1,0:T(8,128)}, f32[256,256]{1,0:T(8,128)}) custom-call(f32[512,256]{1,0:T(8,128)S(1)} %get-tuple-element.6.w_in, f32[256,256]{1,0:T(8,128)S(1)} %get-tuple-element.7.h_in), custom_call_target="tpu_custom_call" | custom-call | tf_op jit(solution)/shard_map/pallas_call | solution.py:411
Async XLA Ops:
  0.6 0.7 %copy-start.1 = (s32[1,1,4,2]{2,3,1,0:T(2,128)S(1)}, s32[1,1,4,2]{2,3,1,0:T(2,128)}, u32[]{:S(2)}) copy-start(s32[1,1,4,2]{2,3,1,0:T(2,128)} %param.6) | copy-start | bytes 100
  0.6 0.7 %copy-start.2 = (s32[1,1,4]{2,1,0:T(1,128)S(1)}, s32[1,1,4]{2,1,0:T(1,128)}, u32[]{:S(2)}) copy-start(s32[1,1,4]{2,1,0:T(1,128)} %param.7) | copy-start | bytes 52
  1.3 0.9 %copy-start = (bf16[256,256]{1,0:T(8,128)(2,1)S(1)}, bf16[256,256]{1,0:T(8,128)(2,1)}, u32[]{:S(2)}) copy-start(bf16[256,256]{1,0:T(8,128)(2,1)} %h_hbm.1) | copy-start | bytes 393220
